TPU v7x, 256 devices: a whole 4x4x8 slice. The times are simulated.
256 devices in a mesh: grid: 16 (over y_hi, z), dom: 16 (over y_lo, x, core).
Axes of the slice: x: 4, y: 4 (y_hi: 2, y_lo: 2; y = y_hi * 2 + y_lo), z: 8, core: 2. Of those that a mesh axis runs over, the one named last changes fastest.
Arguments:
- fields: float32 [16, 64, 16, 16, 256], P('grid', 'dom'), may hold values from -6 to 6
- cutoffs: int32 [16, 4], P('grid'), may hold values from 0 to 2
- weights: int32 [16], P('grid'), may hold values from -3 to 3, as said below
- diffusion: float32 [4], replicated, may hold values from 0.03 to 0.12
- courant: float32 [4], replicated, may hold values from -0.2 to 0.2
Outputs:
- combined_fields: float32 [16, 64, 16, 16, 256], P('grid', 'dom')
Inputs may be any that keep to these rules, and one draw needn't show every extreme that they name: `weights`: each weight is a nonzero integer of magnitude 1 to 3.
All inputs are finite; a program needn't handle non-finite values.
Results may differ from a plain program's by a relative error of at most 0.0003.
Values sent between devices are 32-bit elements; how exact they have to be, the bound alone decides.
A program may use at most 64 MiB of HBM per device.

v0:
```python
import functools
import math

import jax
import jax.numpy as jnp
from jax import lax
from jax.experimental import pallas as pl
from jax.experimental.pallas import tpu as pltpu
from jax.sharding import PartitionSpec as P

SERIES = (1.0, 2.0, 2.0, 4.0 / 3.0, 7.0 / 12.0, 1.0 / 6.0, 1.0 / 36.0)
DEGREE = 6
ROWS = 4
LOW = 6
HIGH = 7
WINDOW = LOW + ROWS + HIGH
RING = 8
MESH = pl.DeviceIdType.MESH
F32 = jnp.float32
BF16 = jnp.bfloat16


def split(x):
    hi = x.astype(BF16)
    return hi, (x - hi.astype(F32)).astype(BF16)


def dot(a, b):
    return jnp.dot(a, b, preferred_element_type=F32)


def fine_surplus(to, source, n):
    ahead = (source - to) & (n - 1)
    near = (ahead == 1) | (ahead == n - 1)
    far = (ahead == 2) | (ahead == n - 2)
    half = ((to & 1) == 1) & near | ((to & 3) == 2) & far
    return jnp.where(ahead == 0, 1.0, jnp.where(half, -0.5, 0.0)).astype(F32)


def fine_restore(to, source, n):
    ahead = (source - to) & (n - 1)
    place = to & 3
    toward = jnp.where(place == 1, ahead, (n - ahead) & (n - 1))
    odd = jnp.where(
        toward == n - 1, 0.75, jnp.where(toward == 1, 0.5, jnp.where(toward == 3, 0.25, 0.0))
    )
    even = jnp.where((place == 2) & ((ahead == 2) | (ahead == n - 2)), 0.5, 0.0)
    return jnp.where(ahead == 0, 1.0, jnp.where((to & 1) == 1, odd, even)).astype(F32)


def coefficients(alpha, beta):
    up, down = [1.0], [1.0]
    for _ in range(DEGREE):
        up.append(up[-1] * alpha)
        down.append(down[-1] * beta)
    q = {}
    for m in range(DEGREE + 1):
        for j in range(m - DEGREE, DEGREE - m + 1):
            total = 0.0
            for l in range(abs(j), DEGREE - m + 1, 2):
                i = (l + j) // 2
                factor = SERIES[m + l] * math.comb(m + l, m) * math.comb(l, i)
                total = total + factor * up[i] * down[l - i]
            q[m, j] = total
    return q


def kernel(
    sizes,
    cutoffs, weights, diffusion, courant, fields, out,
    window, held_a, held_b, product, evolved, surplus, arrived, paired, combined,
    t_hi, t_lo, fine4, fine23, back4, back23, mask23,
    own_sem, low_send, low_recv, high_send, high_recv, plus_send, plus_recv, minus_send, minus_recv,
    pair_send, pair_recv, gplus_send, gplus_recv, gminus_send, gminus_recv, row_send, row_recv,
):
    n2, n3, n4 = sizes
    plane = n2 * n3
    part = ROWS * n2 // (2 * RING)
    half = ROWS * n2 // 2
    grid_at, dom_at = lax.axis_index("grid"), lax.axis_index("dom")
    doms = lax.axis_size("dom")
    above, below = lax.rem(dom_at + 1, doms), lax.rem(dom_at + doms - 1, doms)
    z = lax.rem(grid_at, RING)
    base = grid_at - z
    z_plus, z_minus = base + lax.rem(z + 1, RING), base + lax.rem(z + RING - 1, RING)
    partner = lax.rem(grid_at + RING, 2 * RING)

    barrier = pltpu.get_barrier_semaphore()
    for device in (
        (grid_at, above), (grid_at, below), (z_plus, dom_at), (z_minus, dom_at), (partner, dom_at),
    ):
        pl.semaphore_signal(barrier, inc=1, device_id=device, device_id_type=MESH)
    pl.semaphore_wait(barrier, 5)

    def send(source, target, device, send_sem, recv_sem):
        copy = pltpu.make_async_remote_copy(
            src_ref=source, dst_ref=target, send_sem=send_sem, recv_sem=recv_sem,
            device_id=device, device_id_type=MESH,
        )
        copy.start()
        return copy

    high, low = {}, {}
    for d in range(ROWS):
        high[d] = send(
            fields.at[0, d], window.at[LOW + ROWS + d], (grid_at, below), high_send.at[d], high_recv.at[d]
        )
        low[d] = send(
            fields.at[0, ROWS - 1 - d], window.at[LOW - 1 - d], (grid_at, above), low_send.at[d], low_recv.at[d]
        )
    own = pltpu.make_async_copy(fields.at[0], window.at[LOW : LOW + ROWS], own_sem)
    own.start()

    alpha = [diffusion[d] - courant[d] for d in range(4)]
    beta = [diffusion[d] + courant[d] for d in range(4)]
    centre = -2.0 * (diffusion[0] + diffusion[1] + diffusion[2] + diffusion[3])
    q = coefficients(alpha[0], beta[0])

    source4 = lax.broadcasted_iota(jnp.int32, (n4, n4), 0)
    to4 = lax.broadcasted_iota(jnp.int32, (n4, n4), 1)
    ahead4 = (source4 - to4) & (n4 - 1)
    t = jnp.where(
        ahead4 == 0, centre, jnp.where(ahead4 == 1, alpha[3], jnp.where(ahead4 == n4 - 1, beta[3], 0.0))
    )
    hi, lo = split(t)
    t_hi[...] = hi
    t_lo[...] = lo
    fine4[...] = fine_surplus(to4, source4, n4).astype(BF16)
    back4[...] = fine_restore(to4, source4, n4).astype(BF16)
    to = lax.broadcasted_iota(jnp.int32, (plane, plane), 0)
    source = lax.broadcasted_iota(jnp.int32, (plane, plane), 1)
    shift = n3.bit_length() - 1
    to2, to3, source2, source3 = to >> shift, to & (n3 - 1), source >> shift, source & (n3 - 1)
    fine23[...] = (fine_surplus(to2, source2, n2) * fine_surplus(to3, source3, n3)).astype(BF16)
    back23[...] = (fine_restore(to2, source2, n2) * fine_restore(to3, source3, n3)).astype(BF16)
    line = lax.broadcasted_iota(jnp.int32, (plane, n4), 0)
    cell = lax.broadcasted_iota(jnp.int32, (plane, n4), 1)
    stride = [jnp.left_shift(jnp.int32(1), cutoffs[0, d]) for d in range(4)]
    off = ((line >> shift) & (stride[1] - 1)) | (line & (n3 - 1) & (stride[2] - 1)) | (cell & (stride[3] - 1))
    mask23[...] = jnp.where(off == 0, 1.0, 0.0).astype(F32)
    kept_row = [jnp.where((r & (stride[0] - 1)) == 0, 1.0, 0.0).astype(F32) for r in range(ROWS)]
    weight = weights[0].astype(F32) * (1.0 / (2 * RING))

    own.wait()
    block = 4

    def wait_high(d):
        high[d].wait_recv()
        if d < HIGH - ROWS:
            high[ROWS + d] = send(
                window.at[LOW + ROWS + d], window.at[LOW + 2 * ROWS + d], (grid_at, below),
                high_send.at[ROWS + d], high_recv.at[ROWS + d],
            )

    def wait_low(d):
        low[d].wait_recv()
        if d < LOW - ROWS:
            low[ROWS + d] = send(
                window.at[LOW - 1 - d], window.at[LOW - 1 - ROWS - d], (grid_at, above),
                low_send.at[ROWS + d], low_recv.at[ROWS + d],
            )

    def level(m, now, then):
        def row(r, carry):
            if m < DEGREE:
                flat = now[r, 1 : n2 + 1].reshape(plane, n4)
                hi, lo = split(flat)
                product[...] = dot(hi, t_hi[...]) + dot(lo, t_hi[...]) + dot(hi, t_lo[...])
            for i in range(0, n2, block):
                total = None
                for j in range(m - DEGREE, DEGREE - m + 1):
                    term = q[m, j] * window[LOW + r + j, i : i + block]
                    total = term if total is None else total + term
                if m < DEGREE:
                    here = now[r, i + 1 : i + 1 + block]
                    total = total + product[i * n3 : (i + block) * n3].reshape(block, n3, n4)
                    total = total + alpha[1] * now[r, i + 2 : i + 2 + block] + beta[1] * now[r, i : i + block]
                    total = total + alpha[2] * pltpu.roll(here, n3 - 1, 1) + beta[2] * pltpu.roll(here, 1, 1)
                if m > 0:
                    then[r, i + 1 : i + 1 + block] = total
                else:
                    evolved[r, i : i + block] = total
            if m > 0:
                then[r, 0] = then[r, n2]
                then[r, n2 + 1] = then[r, 1]
            return carry

        lax.fori_loop(0, ROWS + 1, row, 0)

    now, then = held_a, held_b
    for m in range(DEGREE, -1, -1):
        d = DEGREE - m
        wait_high(d)
        if d > 0:
            wait_low(d - 1)
        level(m, now, then)
        now, then = then, now

    def surplus_of(r, flat):
        hi, lo = split(flat)
        flat = dot(hi, fine4[...]) + dot(lo, fine4[...])
        hi, lo = split(flat)
        flat = dot(fine23[...], hi) + dot(fine23[...], lo)
        flat = flat * (mask23[...] * (weight * kept_row[r]))
        surplus[r * n2 : (r + 1) * n2] = flat.reshape(n2, n3, n4)

    def evolved_row(r):
        return evolved[r].reshape(plane, n4)

    surplus_of(0, evolved_row(0))
    surplus_of(1, evolved_row(1) - 0.5 * (evolved_row(0) + evolved_row(2)))
    surplus_of(2, evolved_row(2) - 0.5 * (evolved_row(0) + evolved_row(4)))
    surplus_of(3, evolved_row(3) - 0.5 * (evolved_row(2) + evolved_row(4)))

    def piece(h, offset):
        return pl.ds(h * half + lax.rem(z + offset + RING, RING) * part, part)

    plus_order = [(0, 4), (1, 3), (0, 3), (1, 2), (0, 2), (1, 1), (0, 1)]
    minus_order = [(1 - h, -o) for h, o in plus_order]
    plus, minus = [], []
    for step in range(len(plus_order)):
        for order, copies, slot, device, send_sem, recv_sem in (
            (plus_order, plus, 0, z_plus, plus_send, plus_recv),
            (minus_order, minus, 1, z_minus, minus_send, minus_recv),
        ):
            where = piece(*order[step])
            if step >= 2:
                copies[step - 2].wait_recv()
                surplus[where] = surplus[where] + arrived[slot, step - 2]
            copies.append(
                send(surplus.at[where], arrived.at[slot, step], (device, dom_at), send_sem.at[step], recv_sem.at[step])
            )
    pair = []
    for h in range(2):
        plus[6 - h].wait_recv()
        minus[5 + h].wait_recv()
        mine = piece(h, 0)
        surplus[mine] = surplus[mine] + (arrived[0, 6 - h] + arrived[1, 5 + h])
        pair.append(send(surplus.at[mine], paired.at[h], (partner, dom_at), pair_send.at[h], pair_recv.at[h]))

    gplus_order = [(0, 0), (1, 0), (0, -1), (1, -1), (0, -2), (1, -2), (0, -3)]
    gminus_order = [(1 - h, -o) for h, o in gplus_order]
    gplus, gminus = [], []
    for h in range(2):
        pair[h].wait_recv()
        mine = piece(h, 0)
        combined[mine] = surplus[mine] + paired[h]
    for step in range(len(gplus_order)):
        for order, copies, device, send_sem, recv_sem in (
            (gplus_order, gplus, z_plus, gplus_send, gplus_recv),
            (gminus_order, gminus, z_minus, gminus_send, gminus_recv),
        ):
            if step >= 2:
                copies[step - 2].wait_recv()
            where = piece(*order[step])
            copies.append(
                send(combined.at[where], combined.at[where], (device, dom_at), send_sem.at[step], recv_sem.at[step])
            )
    for copies in (gplus, gminus):
        for step in (5, 6):
            copies[step].wait_recv()

    last = send(
        combined.at[0:n2], combined.at[ROWS * n2 : (ROWS + 1) * n2], (grid_at, below), row_send, row_recv
    )

    def masked(r):
        return combined[r * n2 : (r + 1) * n2].reshape(plane, n4) * mask23[...]

    def restore(r, flat):
        hi, lo = split(flat)
        flat = dot(hi, back4[...]) + dot(lo, back4[...])
        hi, lo = split(flat)
        flat = dot(back23[...], hi) + dot(back23[...], lo)
        out[0, r] = flat.reshape(n2, n3, n4)

    restore(0, masked(0))
    last.wait_recv()
    evolved[4] = masked(4).reshape(n2, n3, n4)
    evolved[2] = (kept_row[2] * masked(2) + 0.5 * (masked(0) + evolved_row(4))).reshape(n2, n3, n4)
    restore(2, evolved_row(2))
    restore(1, kept_row[1] * masked(1) + 0.5 * (masked(0) + evolved_row(2)))
    restore(3, kept_row[3] * masked(3) + 0.5 * (evolved_row(2) + evolved_row(4)))

    for copy in (*high.values(), *low.values(), *plus, *minus, *pair, *gplus, *gminus, last):
        copy.wait_send()


def shards(fields, cutoffs, weights, diffusion, courant):
    n2, n3, n4 = fields.shape[2:]
    plane = n2 * n3
    part = ROWS * n2 // (2 * RING)
    row = (n2, n3, n4)
    dma = pltpu.SemaphoreType.DMA
    return pl.pallas_call(
        functools.partial(kernel, row),
        out_shape=jax.ShapeDtypeStruct(fields.shape, F32),
        in_specs=[pl.BlockSpec(memory_space=pltpu.SMEM)] * 4 + [pl.BlockSpec(memory_space=pl.ANY)],
        out_specs=pl.BlockSpec(memory_space=pltpu.VMEM),
        scratch_shapes=[
            pltpu.VMEM((WINDOW, *row), F32),
            pltpu.VMEM((ROWS + 1, n2 + 2, n3, n4), F32),
            pltpu.VMEM((ROWS + 1, n2 + 2, n3, n4), F32),
            pltpu.VMEM((plane, n4), F32),
            pltpu.VMEM((ROWS + 1, *row), F32),
            pltpu.VMEM((ROWS * n2, n3, n4), F32),
            pltpu.VMEM((2, 7, part, n3, n4), F32),
            pltpu.VMEM((2, part, n3, n4), F32),
            pltpu.VMEM(((ROWS + 1) * n2, n3, n4), F32),
            pltpu.VMEM((n4, n4), BF16),
            pltpu.VMEM((n4, n4), BF16),
            pltpu.VMEM((n4, n4), BF16),
            pltpu.VMEM((plane, plane), BF16),
            pltpu.VMEM((n4, n4), BF16),
            pltpu.VMEM((plane, plane), BF16),
            pltpu.VMEM((plane, n4), F32),
            dma,
            dma((LOW,)), dma((LOW,)), dma((HIGH,)), dma((HIGH,)),
            dma((7,)), dma((7,)), dma((7,)), dma((7,)),
            dma((2,)), dma((2,)),
            dma((7,)), dma((7,)), dma((7,)), dma((7,)),
            dma, dma,
        ],
        compiler_params=pltpu.CompilerParams(
            collective_id=0, has_side_effects=True, vmem_limit_bytes=48 * 1024 * 1024
        ),
        name="advect_combine",
    )(cutoffs, weights, diffusion, courant, fields)


def solution(mesh):
    in_specs = (P("grid", "dom", None, None, None), P("grid", None), P("grid"), P(), P())
    out_specs = P("grid", "dom", None, None, None)
    return jax.shard_map(shards, mesh=mesh, in_specs=in_specs, out_specs=out_specs, check_vma=False)
```

profile of v0, /device:TPU:1, one launch (start us, length us, event | category | flops | bytes accessed | tf_op | source)
XLA Modules:
  0.0 76.8 jit_solution(11151835246506239143)
XLA Ops:
  0.0 0.0 copy-start.3
  0.0 0.0 copy-start.2
  0.0 0.0 copy-start.1
  0.7 0.0 copy-done.3
  0.7 0.0 copy-done.2
  0.7 0.0 copy-done.1
  0.7 0.0 copy-start
  0.7 1.2 %copy-done = f32[1,4,16,16,256]{4,3,2,1,0:T(8,128)S(1)} copy-done((f32[1,4,16,16,256]{4,3,2,1,0:T(8,128)S(1)}, f32[1,4,16,16,256]{4,3,2,1,0:T(8,128)}, u32[]{:S(2)}) %copy-start) | copy-done | bytes 1048600
  2.0 73.9 %advect_combine.1 = f32[1,4,16,16,256]{4,3,2,1,0:T(8,128)S(1)} custom-call(s32[1,4]{1,0:T(1,128)S(1)} %copy-done.1, s32[1]{0:T(128)S(6)} %copy.7.weights, f32[4]{0:T(128)S(1)} %copy-done.2, f32[4]{0:T(128)S(1)} %copy-done.3, f32[1,4,16,16,256]{4,3,2,1,0:T(8,128)S(1)} %copy-done), custom_call_target="tpu_custom_call" | custom-call | tf_op jit(solution)/shard_map/advect_combine/pallas_call | solution.py:295
  75.9 1.0 %copy.8 = f32[1,4,16,16,256]{4,3,2,1,0:T(8,128)} copy(f32[1,4,16,16,256]{4,3,2,1,0:T(8,128)S(1)} %advect_combine.1) | data formatting | bytes 2097152
Async XLA Ops:
  0.0 0.7 copy-start.3
  0.0 0.7 copy-start.2
  0.0 0.7 copy-start.1
  0.7 1.2 %copy-start = (f32[1,4,16,16,256]{4,3,2,1,0:T(8,128)S(1)}, f32[1,4,16,16,256]{4,3,2,1,0:T(8,128)}, u32[]{:S(2)}) copy-start(f32[1,4,16,16,256]{4,3,2,1,0:T(8,128)} %fields.1) | copy-start | bytes 3145732
where the time goes:
time: 76.9 us; the launch traced here: 76.8 us
  Pallas kernels  73.9 us (96%)
  local copies, waits for them, and re-layouts  2.2 us (3%)
    pallas_call x1, Pallas kernels, shards(): pl.pallas_call(functools.partial(kernel, row), out_shape=jax.ShapeDtypeSt...  73.9 us
    unnamed x9, local copies, waits for them, and re-layouts  2.2 us

commit v1 on v0

--- a/solution.py
+++ b/solution.py
@@ -75,8 +75,7 @@
 ):
     n2, n3, n4 = sizes
     plane = n2 * n3
-    part = ROWS * n2 // (2 * RING)
-    half = ROWS * n2 // 2
+    part = n2 // RING
     grid_at, dom_at = lax.axis_index("grid"), lax.axis_index("dom")
     doms = lax.axis_size("dom")
     above, below = lax.rem(dom_at + 1, doms), lax.rem(dom_at + doms - 1, doms)
@@ -160,18 +159,21 @@
                 low_send.at[ROWS + d], low_recv.at[ROWS + d],
             )
 
-    def level(m, now, then):
-        def row(r, carry):
-            if m < DEGREE:
-                flat = now[r, 1 : n2 + 1].reshape(plane, n4)
-                hi, lo = split(flat)
+    def level(d, first, stride, count):
+        m = DEGREE - d
+        now, then = (held_a, held_b) if d % 2 == 0 else (held_b, held_a)
+
+        def row(index, carry):
+            r = first + index * stride
+            if d > 0:
+                hi, lo = split(now[r, 1 : n2 + 1].reshape(plane, n4))
                 product[...] = dot(hi, t_hi[...]) + dot(lo, t_hi[...]) + dot(hi, t_lo[...])
             for i in range(0, n2, block):
                 total = None
-                for j in range(m - DEGREE, DEGREE - m + 1):
+                for j in range(-d, d + 1):
                     term = q[m, j] * window[LOW + r + j, i : i + block]
                     total = term if total is None else total + term
-                if m < DEGREE:
+                if d > 0:
                     here = now[r, i + 1 : i + 1 + block]
                     total = total + product[i * n3 : (i + block) * n3].reshape(block, n3, n4)
                     total = total + alpha[1] * now[r, i + 2 : i + 2 + block] + beta[1] * now[r, i : i + block]
@@ -185,16 +187,20 @@
                 then[r, n2 + 1] = then[r, 1]
             return carry
 
-        lax.fori_loop(0, ROWS + 1, row, 0)
-
-    now, then = held_a, held_b
-    for m in range(DEGREE, -1, -1):
-        d = DEGREE - m
+        if count == 1:
+            row(0, 0)
+        else:
+            lax.fori_loop(0, count, row, 0)
+
+    level(0, 1, 1, 2)
+    for d in range(DEGREE):
+        level(d, 0, 3, 2)
+        level(d + 1, 1, 1, 2)
+        if d > 0:
+            level(d - 1, 4, 1, 1)
         wait_high(d)
-        if d > 0:
-            wait_low(d - 1)
-        level(m, now, then)
-        now, then = then, now
+        wait_low(d)
+    level(DEGREE, 0, 3, 2)
 
     def surplus_of(r, flat):
         hi, lo = split(flat)
@@ -207,62 +213,104 @@
     def evolved_row(r):
         return evolved[r].reshape(plane, n4)
 
+    def piece(c, h, offset):
+        return pl.ds((2 * c + h) * n2 + lax.rem(z + offset + RING, RING) * part, part)
+
+    plus_order = [(0, 4), (1, 3), (0, 3), (1, 2), (0, 2), (1, 1), (0, 1)]
+    minus_order = [(1 - h, -o) for h, o in plus_order]
+    gplus_order = [(0, 0), (1, 0), (0, -1), (1, -1), (0, -2), (1, -2), (0, -3)]
+    gminus_order = [(1 - h, -o) for h, o in gplus_order]
+    steps = len(plus_order)
+    plus, minus, gplus, gminus = [[], []], [[], []], [[], []], [[], []]
+    pair, shifted = [[], []], []
+
+    def scatter_round(c, pace):
+        for step in range(2 * pace, min(2 * pace + 2, steps)):
+            for order, copies, slot, device, send_sem, recv_sem in (
+                (plus_order, plus[c], 0, z_plus, plus_send, plus_recv),
+                (minus_order, minus[c], 1, z_minus, minus_send, minus_recv),
+            ):
+                where = piece(c, *order[step])
+                if step >= 2:
+                    copies[step - 2].wait_recv()
+                    surplus[where] = surplus[where] + arrived[c, slot, step - 2]
+                copies.append(
+                    send(
+                        surplus.at[where], arrived.at[c, slot, step], (device, dom_at),
+                        send_sem.at[c, step], recv_sem.at[c, step],
+                    )
+                )
+
+    def pair_round(c):
+        for h in range(2):
+            plus[c][6 - h].wait_recv()
+            minus[c][5 + h].wait_recv()
+            mine = piece(c, h, 0)
+            surplus[mine] = surplus[mine] + (arrived[c, 0, 6 - h] + arrived[c, 1, 5 + h])
+            pair[c].append(
+                send(surplus.at[mine], paired.at[c, h], (partner, dom_at), pair_send.at[c, h], pair_recv.at[c, h])
+            )
+
+    def shift_row(offset):
+        index = len(shifted)
+        where = piece(0, 0, offset)
+        target = pl.ds(ROWS * n2 + lax.rem(z + offset + RING, RING) * part, part)
+        shifted.append(
+            send(combined.at[where], combined.at[target], (grid_at, below), row_send.at[index], row_recv.at[index])
+        )
+
+    def landed(c, copies, order, step, sign):
+        copies[step].wait_recv()
+        h, offset = order[step]
+        if c == 0 and h == 0:
+            shift_row(offset - sign)
+
+    def gather_round(c, pace):
+        if pace == 0:
+            for h in range(2):
+                pair[c][h].wait_recv()
+                mine = piece(c, h, 0)
+                combined[mine] = surplus[mine] + paired[c, h]
+        for step in range(2 * pace, min(2 * pace + 2, steps)):
+            for order, copies, device, send_sem, recv_sem, sign in (
+                (gplus_order, gplus[c], z_plus, gplus_send, gplus_recv, 1),
+                (gminus_order, gminus[c], z_minus, gminus_send, gminus_recv, -1),
+            ):
+                if step >= 2:
+                    landed(c, copies, order, step - 2, sign)
+                where = piece(c, *order[step])
+                copies.append(
+                    send(
+                        combined.at[where], combined.at[where], (device, dom_at),
+                        send_sem.at[c, step], recv_sem.at[c, step],
+                    )
+                )
+        if pace == 0 and c == 0:
+            shift_row(0)
+
+    def gather_end(c):
+        for step in (5, 6):
+            landed(c, gplus[c], gplus_order, step, 1)
+            landed(c, gminus[c], gminus_order, step, -1)
+
     surplus_of(0, evolved_row(0))
     surplus_of(1, evolved_row(1) - 0.5 * (evolved_row(0) + evolved_row(2)))
+    scatter_round(0, 0)
+    level(DEGREE - 1, 4, 1, 1)
+    wait_high(DEGREE)
+    level(DEGREE, 4, 1, 1)
     surplus_of(2, evolved_row(2) - 0.5 * (evolved_row(0) + evolved_row(4)))
     surplus_of(3, evolved_row(3) - 0.5 * (evolved_row(2) + evolved_row(4)))
-
-    def piece(h, offset):
-        return pl.ds(h * half + lax.rem(z + offset + RING, RING) * part, part)
-
-    plus_order = [(0, 4), (1, 3), (0, 3), (1, 2), (0, 2), (1, 1), (0, 1)]
-    minus_order = [(1 - h, -o) for h, o in plus_order]
-    plus, minus = [], []
-    for step in range(len(plus_order)):
-        for order, copies, slot, device, send_sem, recv_sem in (
-            (plus_order, plus, 0, z_plus, plus_send, plus_recv),
-            (minus_order, minus, 1, z_minus, minus_send, minus_recv),
-        ):
-            where = piece(*order[step])
-            if step >= 2:
-                copies[step - 2].wait_recv()
-                surplus[where] = surplus[where] + arrived[slot, step - 2]
-            copies.append(
-                send(surplus.at[where], arrived.at[slot, step], (device, dom_at), send_sem.at[step], recv_sem.at[step])
-            )
-    pair = []
-    for h in range(2):
-        plus[6 - h].wait_recv()
-        minus[5 + h].wait_recv()
-        mine = piece(h, 0)
-        surplus[mine] = surplus[mine] + (arrived[0, 6 - h] + arrived[1, 5 + h])
-        pair.append(send(surplus.at[mine], paired.at[h], (partner, dom_at), pair_send.at[h], pair_recv.at[h]))
-
-    gplus_order = [(0, 0), (1, 0), (0, -1), (1, -1), (0, -2), (1, -2), (0, -3)]
-    gminus_order = [(1 - h, -o) for h, o in gplus_order]
-    gplus, gminus = [], []
-    for h in range(2):
-        pair[h].wait_recv()
-        mine = piece(h, 0)
-        combined[mine] = surplus[mine] + paired[h]
-    for step in range(len(gplus_order)):
-        for order, copies, device, send_sem, recv_sem in (
-            (gplus_order, gplus, z_plus, gplus_send, gplus_recv),
-            (gminus_order, gminus, z_minus, gminus_send, gminus_recv),
-        ):
-            if step >= 2:
-                copies[step - 2].wait_recv()
-            where = piece(*order[step])
-            copies.append(
-                send(combined.at[where], combined.at[where], (device, dom_at), send_sem.at[step], recv_sem.at[step])
-            )
-    for copies in (gplus, gminus):
-        for step in (5, 6):
-            copies[step].wait_recv()
-
-    last = send(
-        combined.at[0:n2], combined.at[ROWS * n2 : (ROWS + 1) * n2], (grid_at, below), row_send, row_recv
-    )
+    scatter_round(1, 0)
+    for pace in range(1, 4):
+        for c in range(2):
+            scatter_round(c, pace)
+    for c in range(2):
+        pair_round(c)
+    for pace in range(4):
+        for c in range(2):
+            gather_round(c, pace)
+    gather_end(0)
 
     def masked(r):
         return combined[r * n2 : (r + 1) * n2].reshape(plane, n4) * mask23[...]
@@ -275,21 +323,24 @@
         out[0, r] = flat.reshape(n2, n3, n4)
 
     restore(0, masked(0))
-    last.wait_recv()
+    gather_end(1)
+    for copy in shifted:
+        copy.wait_recv()
     evolved[4] = masked(4).reshape(n2, n3, n4)
     evolved[2] = (kept_row[2] * masked(2) + 0.5 * (masked(0) + evolved_row(4))).reshape(n2, n3, n4)
     restore(2, evolved_row(2))
     restore(1, kept_row[1] * masked(1) + 0.5 * (masked(0) + evolved_row(2)))
     restore(3, kept_row[3] * masked(3) + 0.5 * (evolved_row(2) + evolved_row(4)))
 
-    for copy in (*high.values(), *low.values(), *plus, *minus, *pair, *gplus, *gminus, last):
+    rings = [copy for copies in (plus, minus, pair, gplus, gminus) for chunk in copies for copy in chunk]
+    for copy in (*high.values(), *low.values(), *rings, *shifted):
         copy.wait_send()
 
 
 def shards(fields, cutoffs, weights, diffusion, courant):
     n2, n3, n4 = fields.shape[2:]
     plane = n2 * n3
-    part = ROWS * n2 // (2 * RING)
+    part = n2 // RING
     row = (n2, n3, n4)
     dma = pltpu.SemaphoreType.DMA
     return pl.pallas_call(
@@ -304,8 +355,8 @@
             pltpu.VMEM((plane, n4), F32),
             pltpu.VMEM((ROWS + 1, *row), F32),
             pltpu.VMEM((ROWS * n2, n3, n4), F32),
-            pltpu.VMEM((2, 7, part, n3, n4), F32),
-            pltpu.VMEM((2, part, n3, n4), F32),
+            pltpu.VMEM((2, 2, 7, part, n3, n4), F32),
+            pltpu.VMEM((2, 2, part, n3, n4), F32),
             pltpu.VMEM(((ROWS + 1) * n2, n3, n4), F32),
             pltpu.VMEM((n4, n4), BF16),
             pltpu.VMEM((n4, n4), BF16),
@@ -316,13 +367,13 @@
             pltpu.VMEM((plane, n4), F32),
             dma,
             dma((LOW,)), dma((LOW,)), dma((HIGH,)), dma((HIGH,)),
-            dma((7,)), dma((7,)), dma((7,)), dma((7,)),
-            dma((2,)), dma((2,)),
-            dma((7,)), dma((7,)), dma((7,)), dma((7,)),
-            dma, dma,
+            dma((2, 7)), dma((2, 7)), dma((2, 7)), dma((2, 7)),
+            dma((2, 2)), dma((2, 2)),
+            dma((2, 7)), dma((2, 7)), dma((2, 7)), dma((2, 7)),
+            dma((8,)), dma((8,)),
         ],
         compiler_params=pltpu.CompilerParams(
-            collective_id=0, has_side_effects=True, vmem_limit_bytes=48 * 1024 * 1024
+            collective_id=0, has_side_effects=True, vmem_limit_bytes=60 * 1024 * 1024
         ),
         name="advect_combine",
     )(cutoffs, weights, diffusion, courant, fields)

time: 76.9 us -> 69.7 us (0.906)
  Pallas kernels: 73.9 us -> 66.3 us
    pallas_call x1, Pallas kernels: 73.9 us -> 66.3 us  [shards(): pl.pallas_call(functools.partial(kernel, row), out_shape=jax.ShapeDtypeSt...]
    unnamed x9 -> x1, local copies, waits for them, and re-layouts: 2.2 us -> 2.26 us
where the time goes in v1:
time: 69.7 us; the launch traced here: 69.3 us
  Pallas kernels  66.3 us (95%)
  local copies, waits for them, and re-layouts  2.26 us (3%)
    pallas_call x1, Pallas kernels, shards(): pl.pallas_call(functools.partial(kernel, row), out_shape=jax.ShapeDtypeSt...  66.3 us
    unnamed x1, local copies, waits for them, and re-layouts  2.26 us

profile of v1, /device:TPU:1, one launch (start us, length us, event | category | flops | bytes accessed | tf_op | source)
XLA Modules:
  0.0 69.3 jit_solution(10945687372012084919)
XLA Ops:
  0.7 66.3 %advect_combine.1 = f32[1,4,16,16,256]{4,3,2,1,0:T(8,128)} custom-call(s32[1,4]{1,0:T(1,128)} %cutoffs.1, s32[1]{0:T(128)S(6)} %copy.7.weights, f32[4]{0:T(128)} %diffusion.1, f32[4]{0:T(128)} %courant.1, f32[1,4,16,16,256]{4,3,2,1,0:T(8,128)} %fields.1), custom_call_target="tpu_custom_call" | custom-call | tf_op jit(solution)/shard_map/advect_combine/pallas_call | solution.py:346
  67.0 2.3 %copy.8 = f32[1,4,16,16,256]{4,3,2,1,0:T(8,128)} copy(f32[1,4,16,16,256]{4,3,2,1,0:T(8,128)} %advect_combine.1) | data formatting | bytes 2097152

commit v2 on v1

--- a/solution.py
+++ b/solution.py
@@ -68,10 +68,11 @@
 def kernel(
     sizes,
     cutoffs, weights, diffusion, courant, fields, out,
-    window, held_a, held_b, product, evolved, surplus, arrived, paired, combined,
+    window, held_a, held_b, product, evolved, surplus, arrived, last, paired, combined,
     t_hi, t_lo, fine4, fine23, back4, back23, mask23,
-    own_sem, low_send, low_recv, high_send, high_recv, plus_send, plus_recv, minus_send, minus_recv,
-    pair_send, pair_recv, gplus_send, gplus_recv, gminus_send, gminus_recv, row_send, row_recv,
+    own_sem, low_send, low_recv, high_send, high_recv,
+    ring_send, ring_recv, last_send, last_recv, pair_send, pair_recv,
+    first_send, first_recv, gpair_send, gpair_recv, gring_send, gring_recv, row_send, row_recv,
 ):
     n2, n3, n4 = sizes
     plane = n2 * n3
@@ -81,15 +82,19 @@
     above, below = lax.rem(dom_at + 1, doms), lax.rem(dom_at + doms - 1, doms)
     z = lax.rem(grid_at, RING)
     base = grid_at - z
-    z_plus, z_minus = base + lax.rem(z + 1, RING), base + lax.rem(z + RING - 1, RING)
-    partner = lax.rem(grid_at + RING, 2 * RING)
+    other = lax.rem(base + RING, 2 * RING)
+    z_next = (lax.rem(z + 1, RING), lax.rem(z + RING - 1, RING))
+    beside = [((base + at, dom_at), (other + at, dom_at)) for at in z_next]
+    partner = (other + z, dom_at)
+    y = base // RING
+    y_other = 1 - y
 
     barrier = pltpu.get_barrier_semaphore()
-    for device in (
-        (grid_at, above), (grid_at, below), (z_plus, dom_at), (z_minus, dom_at), (partner, dom_at),
-    ):
+    for device in ((grid_at, above), (grid_at, below), *beside[0], *beside[1], partner):
         pl.semaphore_signal(barrier, inc=1, device_id=device, device_id_type=MESH)
-    pl.semaphore_wait(barrier, 5)
+    own = pltpu.make_async_copy(fields.at[0], window.at[LOW : LOW + ROWS], own_sem)
+    own.start()
+    pl.semaphore_wait(barrier, 7)
 
     def send(source, target, device, send_sem, recv_sem):
         copy = pltpu.make_async_remote_copy(
@@ -107,9 +112,6 @@
         low[d] = send(
             fields.at[0, ROWS - 1 - d], window.at[LOW - 1 - d], (grid_at, above), low_send.at[d], low_recv.at[d]
         )
-    own = pltpu.make_async_copy(fields.at[0], window.at[LOW : LOW + ROWS], own_sem)
-    own.start()
-
     alpha = [diffusion[d] - courant[d] for d in range(4)]
     beta = [diffusion[d] + courant[d] for d in range(4)]
     centre = -2.0 * (diffusion[0] + diffusion[1] + diffusion[2] + diffusion[3])
@@ -216,40 +218,51 @@
     def piece(c, h, offset):
         return pl.ds((2 * c + h) * n2 + lax.rem(z + offset + RING, RING) * part, part)
 
-    plus_order = [(0, 4), (1, 3), (0, 3), (1, 2), (0, 2), (1, 1), (0, 1)]
-    minus_order = [(1 - h, -o) for h, o in plus_order]
-    gplus_order = [(0, 0), (1, 0), (0, -1), (1, -1), (0, -2), (1, -2), (0, -3)]
-    gminus_order = [(1 - h, -o) for h, o in gplus_order]
-    steps = len(plus_order)
-    plus, minus, gplus, gminus = [[], []], [[], []], [[], []], [[], []]
-    pair, shifted = [[], []], []
+    def layer(c, h, offset, at):
+        return pl.ds((2 * c + h) * n2 + lax.rem(z + offset + RING, RING) * part + at, 1)
+
+    order = [[(0, 4), (1, 3), (0, 3), (1, 2), (0, 2), (1, 1), (0, 1)]]
+    order.append([(1 - h, -o) for h, o in order[0]])
+    gorder = [[(0, 0), (1, 0), (0, -1), (1, -1), (0, -2), (1, -2), (0, -3)]]
+    gorder.append([(1 - h, -o) for h, o in gorder[0]])
+    steps, inner = len(order[0]), len(order[0]) - 2
+    ring, ends, pairs, first, gpairs, gring, shifted = {}, {}, {}, {}, {}, {}, []
 
     def scatter_round(c, pace):
         for step in range(2 * pace, min(2 * pace + 2, steps)):
-            for order, copies, slot, device, send_sem, recv_sem in (
-                (plus_order, plus[c], 0, z_plus, plus_send, plus_recv),
-                (minus_order, minus[c], 1, z_minus, minus_send, minus_recv),
-            ):
-                where = piece(c, *order[step])
+            for way in range(2):
+                h, offset = order[way][step]
+                where = piece(c, h, offset)
                 if step >= 2:
-                    copies[step - 2].wait_recv()
-                    surplus[where] = surplus[where] + arrived[c, slot, step - 2]
-                copies.append(
-                    send(
-                        surplus.at[where], arrived.at[c, slot, step], (device, dom_at),
-                        send_sem.at[c, step], recv_sem.at[c, step],
+                    ring[c, way, step - 2].wait_recv()
+                    surplus[where] = surplus[where] + arrived[c, way, step - 2]
+                if step < inner:
+                    ring[c, way, step] = send(
+                        surplus.at[where], arrived.at[c, way, step], beside[way][0],
+                        ring_send.at[c, way, step], ring_recv.at[c, way, step],
                     )
+                    continue
+                for across, at in ((1, y_other), (0, y)):
+                    ends[c, way, h, across] = send(
+                        surplus.at[layer(c, h, offset, at)], last.at[c, way, h, across], beside[way][across],
+                        last_send.at[c, way, h, across], last_recv.at[c, way, h, across],
+                    )
+        if pace == 0:
+            for h in range(2):
+                pairs[c, h] = send(
+                    surplus.at[layer(c, h, 0, y_other)], paired.at[c, h], partner,
+                    pair_send.at[c, h], pair_recv.at[c, h],
                 )
 
-    def pair_round(c):
-        for h in range(2):
-            plus[c][6 - h].wait_recv()
-            minus[c][5 + h].wait_recv()
-            mine = piece(c, h, 0)
-            surplus[mine] = surplus[mine] + (arrived[c, 0, 6 - h] + arrived[c, 1, 5 + h])
-            pair[c].append(
-                send(surplus.at[mine], paired.at[c, h], (partner, dom_at), pair_send.at[c, h], pair_recv.at[c, h])
-            )
+    def finish(c, h):
+        pairs[c, h].wait_recv()
+        mine = layer(c, h, 0, y)
+        total = surplus[mine] + paired[c, h]
+        for across in range(2):
+            for way in range(2):
+                ends[c, way, h, across].wait_recv()
+            total = total + (last[c, 0, h, across] + last[c, 1, h, across])
+        combined[mine] = total
 
     def shift_row(offset):
         index = len(shifted)
@@ -259,39 +272,46 @@
             send(combined.at[where], combined.at[target], (grid_at, below), row_send.at[index], row_recv.at[index])
         )
 
-    def landed(c, copies, order, step, sign):
-        copies[step].wait_recv()
-        h, offset = order[step]
+    def landed(c, way, step):
+        h, offset = gorder[way][step]
+        if step < 2:
+            for across in range(2):
+                first[c, way, h, across].wait_recv()
+        else:
+            gring[c, way, step - 2].wait_recv()
         if c == 0 and h == 0:
-            shift_row(offset - sign)
+            shift_row(offset - (1 - 2 * way))
 
     def gather_round(c, pace):
         if pace == 0:
             for h in range(2):
-                pair[c][h].wait_recv()
-                mine = piece(c, h, 0)
-                combined[mine] = surplus[mine] + paired[c, h]
+                finish(c, h)
+                mine = combined.at[layer(c, h, 0, y)]
+                for across in (1, 0):
+                    for way in range(2):
+                        first[c, way, h, across] = send(
+                            mine, mine, beside[way][across],
+                            first_send.at[c, way, h, across], first_recv.at[c, way, h, across],
+                        )
+                gpairs[c, h] = send(mine, mine, partner, gpair_send.at[c, h], gpair_recv.at[c, h])
+            return
         for step in range(2 * pace, min(2 * pace + 2, steps)):
-            for order, copies, device, send_sem, recv_sem, sign in (
-                (gplus_order, gplus[c], z_plus, gplus_send, gplus_recv, 1),
-                (gminus_order, gminus[c], z_minus, gminus_send, gminus_recv, -1),
-            ):
-                if step >= 2:
-                    landed(c, copies, order, step - 2, sign)
-                where = piece(c, *order[step])
-                copies.append(
-                    send(
-                        combined.at[where], combined.at[where], (device, dom_at),
-                        send_sem.at[c, step], recv_sem.at[c, step],
-                    )
+            for way in range(2):
+                landed(c, way, step - 2)
+                where = combined.at[piece(c, *gorder[way][step])]
+                gring[c, way, step - 2] = send(
+                    where, where, beside[way][0], gring_send.at[c, way, step - 2], gring_recv.at[c, way, step - 2]
                 )
-        if pace == 0 and c == 0:
-            shift_row(0)
+        if pace == 1:
+            for h in range(2):
+                gpairs[c, h].wait_recv()
+            if c == 0:
+                shift_row(0)
 
     def gather_end(c):
-        for step in (5, 6):
-            landed(c, gplus[c], gplus_order, step, 1)
-            landed(c, gminus[c], gminus_order, step, -1)
+        for step in (inner, inner + 1):
+            for way in range(2):
+                landed(c, way, step)
 
     surplus_of(0, evolved_row(0))
     surplus_of(1, evolved_row(1) - 0.5 * (evolved_row(0) + evolved_row(2)))
@@ -305,8 +325,6 @@
     for pace in range(1, 4):
         for c in range(2):
             scatter_round(c, pace)
-    for c in range(2):
-        pair_round(c)
     for pace in range(4):
         for c in range(2):
             gather_round(c, pace)
@@ -332,8 +350,8 @@
     restore(1, kept_row[1] * masked(1) + 0.5 * (masked(0) + evolved_row(2)))
     restore(3, kept_row[3] * masked(3) + 0.5 * (evolved_row(2) + evolved_row(4)))
 
-    rings = [copy for copies in (plus, minus, pair, gplus, gminus) for chunk in copies for copy in chunk]
-    for copy in (*high.values(), *low.values(), *rings, *shifted):
+    started = (high, low, ring, ends, pairs, first, gpairs, gring)
+    for copy in (*(copy for group in started for copy in group.values()), *shifted):
         copy.wait_send()
 
 
@@ -355,8 +373,9 @@
             pltpu.VMEM((plane, n4), F32),
             pltpu.VMEM((ROWS + 1, *row), F32),
             pltpu.VMEM((ROWS * n2, n3, n4), F32),
-            pltpu.VMEM((2, 2, 7, part, n3, n4), F32),
-            pltpu.VMEM((2, 2, part, n3, n4), F32),
+            pltpu.VMEM((2, 2, 5, part, n3, n4), F32),
+            pltpu.VMEM((2, 2, 2, 2, 1, n3, n4), F32),
+            pltpu.VMEM((2, 2, 1, n3, n4), F32),
             pltpu.VMEM(((ROWS + 1) * n2, n3, n4), F32),
             pltpu.VMEM((n4, n4), BF16),
             pltpu.VMEM((n4, n4), BF16),
@@ -365,15 +384,13 @@
             pltpu.VMEM((n4, n4), BF16),
             pltpu.VMEM((plane, plane), BF16),
             pltpu.VMEM((plane, n4), F32),
-            dma,
-            dma((LOW,)), dma((LOW,)), dma((HIGH,)), dma((HIGH,)),
-            dma((2, 7)), dma((2, 7)), dma((2, 7)), dma((2, 7)),
-            dma((2, 2)), dma((2, 2)),
-            dma((2, 7)), dma((2, 7)), dma((2, 7)), dma((2, 7)),
+            dma, dma((LOW,)), dma((LOW,)), dma((HIGH,)), dma((HIGH,)),
+            dma((2, 2, 5)), dma((2, 2, 5)), dma((2, 2, 2, 2)), dma((2, 2, 2, 2)), dma((2, 2)), dma((2, 2)),
+            dma((2, 2, 2, 2)), dma((2, 2, 2, 2)), dma((2, 2)), dma((2, 2)), dma((2, 2, 5)), dma((2, 2, 5)),
             dma((8,)), dma((8,)),
         ],
         compiler_params=pltpu.CompilerParams(
-            collective_id=0, has_side_effects=True, vmem_limit_bytes=60 * 1024 * 1024
+            collective_id=0, has_side_effects=True, vmem_limit_bytes=52 * 1024 * 1024
         ),
         name="advect_combine",
     )(cutoffs, weights, diffusion, courant, fields)

time: 69.7 us -> 67.2 us (0.964)
  Pallas kernels: 66.3 us -> 64.5 us
  local copies, waits for them, and re-layouts: 2.26 us -> 0.98 us
    pallas_call x1, Pallas kernels: 66.3 us -> 64.5 us  [shards(): pl.pallas_call(functools.partial(kernel, row), out_shape=jax.ShapeDtypeSt...]
    unnamed x1 -> x7, local copies, waits for them, and re-layouts: 2.26 us -> 0.98 us
where the time goes in v2:
time: 67.2 us; the launch traced here: 66.2 us
  Pallas kernels  64.5 us (96%)
  local copies, waits for them, and re-layouts  0.98 us (1%)
  between operations  0.73 us (1%)
    pallas_call x1, Pallas kernels, shards(): pl.pallas_call(functools.partial(kernel, row), out_shape=jax.ShapeDtypeSt...  64.5 us

profile of v2, /device:TPU:1, one launch (start us, length us, event | category | flops | bytes accessed | tf_op | source)
XLA Modules:
  0.0 66.2 jit_solution(5222319291777762995)
XLA Ops:
  0.0 0.0 copy-start.2
  0.0 0.0 copy-start.1
  0.0 0.0 copy-start
  0.7 0.0 copy-done.2
  0.7 0.0 copy-done.1
  0.7 0.0 copy-done
  0.7 64.5 %advect_combine.1 = f32[1,4,16,16,256]{4,3,2,1,0:T(8,128)S(1)} custom-call(s32[1,4]{1,0:T(1,128)S(1)} %copy-done, s32[1]{0:T(128)S(6)} %copy.7.weights, f32[4]{0:T(128)S(1)} %copy-done.1, f32[4]{0:T(128)S(1)} %copy-done.2, f32[1,4,16,16,256]{4,3,2,1,0:T(8,128)} %fields.1), custom_call_target="tpu_custom_call" | custom-call | tf_op jit(solution)/shard_map/advect_combine/pallas_call | solution.py:364
  65.2 1.0 %copy.8 = f32[1,4,16,16,256]{4,3,2,1,0:T(8,128)} copy(f32[1,4,16,16,256]{4,3,2,1,0:T(8,128)S(1)} %advect_combine.1) | data formatting | bytes 2097152
Async XLA Ops:
  0.0 0.7 %copy-start.2 = (f32[4]{0:T(128)S(1)}, f32[4]{0:T(128)}, u32[]{:S(2)}) copy-start(f32[4]{0:T(128)} %courant.1) | copy-start | bytes 52
  0.0 0.7 %copy-start.1 = (f32[4]{0:T(128)S(1)}, f32[4]{0:T(128)}, u32[]{:S(2)}) copy-start(f32[4]{0:T(128)} %diffusion.1) | copy-start | bytes 52
  0.0 0.7 %copy-start = (s32[1,4]{1,0:T(1,128)S(1)}, s32[1,4]{1,0:T(1,128)}, u32[]{:S(2)}) copy-start(s32[1,4]{1,0:T(1,128)} %cutoffs.1) | copy-start | bytes 52

commit v3 on v2

v3 whole, which is shorter than its diff:
```python
import functools
import math

import jax
import jax.numpy as jnp
from jax import lax
from jax.experimental import pallas as pl
from jax.experimental.pallas import tpu as pltpu
from jax.sharding import PartitionSpec as P

SERIES = (1.0, 2.0, 2.0, 4.0 / 3.0, 7.0 / 12.0, 1.0 / 6.0, 1.0 / 36.0)
DEGREE = 6
ROWS = 4
LOW = 6
HIGH = 7
WINDOW = LOW + ROWS + HIGH
RING = 8
SIGNS = (1.0, -1.0)
MESH = pl.DeviceIdType.MESH
F32 = jnp.float32
BF16 = jnp.bfloat16


def split(x):
    hi = x.astype(BF16)
    return hi, (x - hi.astype(F32)).astype(BF16)


def dot(a, b):
    return jnp.dot(a, b, preferred_element_type=F32)


def fine_surplus(to, source, n):
    ahead = (source - to) & (n - 1)
    near = (ahead == 1) | (ahead == n - 1)
    far = (ahead == 2) | (ahead == n - 2)
    half = ((to & 1) == 1) & near | ((to & 3) == 2) & far
    return jnp.where(ahead == 0, 1.0, jnp.where(half, -0.5, 0.0)).astype(F32)


def fine_restore(to, source, n):
    ahead = (source - to) & (n - 1)
    place = to & 3
    toward = jnp.where(place == 1, ahead, (n - ahead) & (n - 1))
    odd = jnp.where(
        toward == n - 1, 0.75, jnp.where(toward == 1, 0.5, jnp.where(toward == 3, 0.25, 0.0))
    )
    even = jnp.where((place == 2) & ((ahead == 2) | (ahead == n - 2)), 0.5, 0.0)
    return jnp.where(ahead == 0, 1.0, jnp.where((to & 1) == 1, odd, even)).astype(F32)


def coefficients(alpha, beta):
    up, down = [1.0], [1.0]
    for _ in range(DEGREE):
        up.append(up[-1] * alpha)
        down.append(down[-1] * beta)
    q = {}
    for m in range(DEGREE + 1):
        for j in range(m - DEGREE, DEGREE - m + 1):
            total = 0.0
            for l in range(abs(j), DEGREE - m + 1, 2):
                i = (l + j) // 2
                factor = SERIES[m + l] * math.comb(m + l, m) * math.comb(l, i)
                total = total + factor * up[i] * down[l - i]
            q[m, j] = total
    return q


def kernel(
    sizes,
    cutoffs, weights, diffusion, courant, fields, out,
    raw, window, held_a, held_b, product, evolved, surplus, arrived, last, paired, combined, next_row, restored,
    t_hi, t_lo, fine4, fine23, back4, back23, mask23,
    own_sem, low_send, low_recv, high_send, high_recv,
    ring_send, ring_recv, last_send, last_recv, pair_send, pair_recv,
    first_send, first_recv, gpair_send, gpair_recv, gring_send, gring_recv, row_send, row_recv,
):
    n2, n3, n4 = sizes
    half = n2 // 2
    plane = half * n3
    split_shape = (half, 2, n3 // 2, n4)
    grid_at, dom_at = lax.axis_index("grid"), lax.axis_index("dom")
    doms = lax.axis_size("dom")
    above, below = lax.rem(dom_at + 1, doms), lax.rem(dom_at + doms - 1, doms)
    z = lax.rem(grid_at, RING)
    base = grid_at - z
    other = lax.rem(base + RING, 2 * RING)
    z_next = (lax.rem(z + 1, RING), lax.rem(z + RING - 1, RING))
    beside = [((base + at, dom_at), (other + at, dom_at)) for at in z_next]
    partner = (other + z, dom_at)
    y = base // RING
    y_other = 1 - y

    barrier = pltpu.get_barrier_semaphore()
    for device in ((grid_at, above), (grid_at, below), *beside[0], *beside[1], partner):
        pl.semaphore_signal(barrier, inc=1, device_id=device, device_id_type=MESH)
    own = pltpu.make_async_copy(fields.at[0], raw, own_sem)
    own.start()
    own.wait()
    for r in range(ROWS):
        for c, sign in enumerate(SIGNS):
            window[c, LOW + r] = raw[r, :half] + sign * raw[r, half:]
    pl.semaphore_wait(barrier, 7)

    def send(source, target, device, send_sem, recv_sem):
        copy = pltpu.make_async_remote_copy(
            src_ref=source, dst_ref=target, send_sem=send_sem, recv_sem=recv_sem,
            device_id=device, device_id_type=MESH,
        )
        copy.start()
        return copy

    high, low = {}, {}

    def send_high(c, d, source):
        high[c, d] = send(
            window.at[c, source], window.at[c, LOW + ROWS + d], (grid_at, below), high_send.at[c, d], high_recv.at[c, d]
        )

    def send_low(c, d, source):
        low[c, d] = send(
            window.at[c, source], window.at[c, LOW - 1 - d], (grid_at, above), low_send.at[c, d], low_recv.at[c, d]
        )

    def send_own(c):
        for d in range(ROWS):
            send_high(c, d, LOW + d)
            send_low(c, d, LOW + ROWS - 1 - d)

    def wait_high(c, d):
        high[c, d].wait_recv()
        if d < HIGH - ROWS:
            send_high(c, ROWS + d, LOW + ROWS + d)

    def wait_low(c, d):
        low[c, d].wait_recv()
        if d < LOW - ROWS:
            send_low(c, ROWS + d, LOW - 1 - d)

    send_own(0)

    alpha = [diffusion[d] - courant[d] for d in range(4)]
    beta = [diffusion[d] + courant[d] for d in range(4)]
    centre = -2.0 * (diffusion[0] + diffusion[1] + diffusion[2] + diffusion[3])
    q = coefficients(alpha[0], beta[0])

    source4 = lax.broadcasted_iota(jnp.int32, (n4, n4), 0)
    to4 = lax.broadcasted_iota(jnp.int32, (n4, n4), 1)
    ahead4 = (source4 - to4) & (n4 - 1)
    t = jnp.where(
        ahead4 == 0, centre, jnp.where(ahead4 == 1, alpha[3], jnp.where(ahead4 == n4 - 1, beta[3], 0.0))
    )
    hi, lo = split(t)
    t_hi[...] = hi
    t_lo[...] = lo
    fine4[...] = fine_surplus(to4, source4, n4).astype(BF16)
    back4[...] = fine_restore(to4, source4, n4).astype(BF16)
    to = lax.broadcasted_iota(jnp.int32, (plane, plane), 0)
    source = lax.broadcasted_iota(jnp.int32, (plane, plane), 1)
    shift = n3.bit_length() - 1
    to2, to3, source2, source3 = to >> shift, to & (n3 - 1), source >> shift, source & (n3 - 1)
    fine = fine_surplus(to2, source2, half) * fine_surplus(to3, source3, n3)
    back = fine_restore(to2, source2, half) * fine_restore(to3, source3, n3)
    wraps = (source2 == 0) & (to2 > half // 2)
    for c, sign in enumerate(SIGNS):
        fine23[c] = jnp.where(wraps, sign * fine, fine).astype(BF16)
        back23[c] = jnp.where(wraps, sign * back, back).astype(BF16)
    line = lax.broadcasted_iota(jnp.int32, (plane, n4), 0)
    cell = lax.broadcasted_iota(jnp.int32, (plane, n4), 1)
    stride = [jnp.left_shift(jnp.int32(1), cutoffs[0, d]) for d in range(4)]
    off = ((line >> shift) & (stride[1] - 1)) | (line & (n3 - 1) & (stride[2] - 1)) | (cell & (stride[3] - 1))
    mask23[...] = jnp.where(off == 0, 1.0, 0.0).astype(F32)
    kept_row = [jnp.where((r & (stride[0] - 1)) == 0, 1.0, 0.0).astype(F32) for r in range(ROWS)]
    weight = weights[0].astype(F32) * (0.5 / (2 * RING))

    block = 4

    def level(c, d, first_row, stride_row, count):
        m = DEGREE - d
        now, then = (held_a, held_b) if d % 2 == 0 else (held_b, held_a)

        def row(index, carry):
            r = first_row + index * stride_row
            if d > 0:
                hi, lo = split(now[r, 1 : half + 1].reshape(plane, n4))
                product[...] = dot(hi, t_hi[...]) + dot(lo, t_hi[...]) + dot(hi, t_lo[...])
            for i in range(0, half, block):
                total = None
                for j in range(-d, d + 1):
                    term = q[m, j] * window[c, LOW + r + j, i : i + block]
                    total = term if total is None else total + term
                if d > 0:
                    here = now[r, i + 1 : i + 1 + block]
                    total = total + product[i * n3 : (i + block) * n3].reshape(block, n3, n4)
                    total = total + alpha[1] * now[r, i + 2 : i + 2 + block] + beta[1] * now[r, i : i + block]
                    total = total + alpha[2] * pltpu.roll(here, n3 - 1, 1) + beta[2] * pltpu.roll(here, 1, 1)
                if m > 0:
                    then[r, i + 1 : i + 1 + block] = total
                else:
                    evolved[r, i : i + block] = total
            if m > 0:
                then[r, 0] = SIGNS[c] * then[r, half]
                then[r, half + 1] = SIGNS[c] * then[r, 1]
            return carry

        if count == 1:
            row(0, 0)
        else:
            lax.fori_loop(0, count, row, 0)

    def evolve_start(c):
        level(c, 0, 1, 1, 2)

    def evolve_step(c, d):
        level(c, d, 0, 3, 2)
        level(c, d + 1, 1, 1, 2)
        if d > 0:
            level(c, d - 1, 4, 1, 1)
        wait_high(c, d)
        wait_low(c, d)

    def evolve_end(c):
        level(c, DEGREE, 0, 3, 2)
        level(c, DEGREE - 1, 4, 1, 1)
        surplus_of(c, 0, evolved_row(0))
        surplus_of(c, 1, evolved_row(1) - 0.5 * (evolved_row(0) + evolved_row(2)))
        wait_high(c, DEGREE)
        level(c, DEGREE, 4, 1, 1)
        surplus_of(c, 2, evolved_row(2) - 0.5 * (evolved_row(0) + evolved_row(4)))
        surplus_of(c, 3, evolved_row(3) - 0.5 * (evolved_row(2) + evolved_row(4)))

    def surplus_of(c, r, flat):
        hi, lo = split(flat)
        flat = dot(hi, fine4[...]) + dot(lo, fine4[...])
        hi, lo = split(flat)
        flat = dot(fine23[c], hi) + dot(fine23[c], lo)
        flat = flat * (mask23[...] * (weight * kept_row[r]))
        surplus[c, r % 2, :, :, r // 2] = flat.reshape(split_shape)

    def evolved_row(r):
        return evolved[r].reshape(plane, n4)

    def at_z(offset):
        return lax.rem(z + offset + RING, RING)

    order = [[(0, 4), (1, 3), (0, 3), (1, 2), (0, 2), (1, 1), (0, 1)]]
    order.append([(1 - h, -o) for h, o in order[0]])
    gorder = [[(0, 0), (1, 0), (0, -1), (1, -1), (0, -2), (1, -2), (0, -3)]]
    gorder.append([(1 - h, -o) for h, o in gorder[0]])
    steps, inner = len(order[0]), len(order[0]) - 2
    ring, ends, pairs, first, gpairs, gring, shifted = {}, {}, {}, {}, {}, {}, ({}, {})

    def scatter_round(c, pace):
        for step in range(2 * pace, min(2 * pace + 2, steps)):
            for way in range(2):
                h, offset = order[way][step]
                where = at_z(offset)
                if step >= 2:
                    ring[c, way, step - 2].wait_recv()
                    surplus[c, h, where] = surplus[c, h, where] + arrived[c, way, step - 2]
                if step < inner:
                    ring[c, way, step] = send(
                        surplus.at[c, h, where], arrived.at[c, way, step], beside[way][0],
                        ring_send.at[c, way, step], ring_recv.at[c, way, step],
                    )
                    continue
                for across, part in ((1, y_other), (0, y)):
                    ends[c, way, h, across] = send(
                        surplus.at[c, h, where, part], last.at[c, way, h, across], beside[way][across],
                        last_send.at[c, way, h, across], last_recv.at[c, way, h, across],
                    )
        if pace == 0:
            for h in range(2):
                pairs[c, h] = send(
                    surplus.at[c, h, z, y_other], paired.at[c, h], partner, pair_send.at[c, h], pair_recv.at[c, h]
                )

    def finish(c, h):
        pairs[c, h].wait_recv()
        total = surplus[c, h, z, y] + paired[c, h]
        for across in range(2):
            for way in range(2):
                ends[c, way, h, across].wait_recv()
            total = total + (last[c, 0, h, across] + last[c, 1, h, across])
        combined[c, h, z, y] = total

    def shift_row(c, offset):
        index = len(shifted[c])
        where = at_z(offset)
        shifted[c][index] = send(
            combined.at[c, 0, where, :, 0], next_row.at[c, where], (grid_at, below),
            row_send.at[c, index], row_recv.at[c, index],
        )

    def landed(c, way, step):
        h, offset = gorder[way][step]
        if step < 2:
            for across in range(2):
                first[c, way, h, across].wait_recv()
        else:
            gring[c, way, step - 2].wait_recv()
        if h == 0:
            shift_row(c, offset - (1 - 2 * way))

    def gather_round(c, pace):
        if pace == 0:
            for h in range(2):
                finish(c, h)
                mine = combined.at[c, h, z, y]
                for across in (1, 0):
                    for way in range(2):
                        first[c, way, h, across] = send(
                            mine, mine, beside[way][across],
                            first_send.at[c, way, h, across], first_recv.at[c, way, h, across],
                        )
                gpairs[c, h] = send(mine, mine, partner, gpair_send.at[c, h], gpair_recv.at[c, h])
            return
        for step in range(2 * pace, min(2 * pace + 2, steps)):
            for way in range(2):
                landed(c, way, step - 2)
                h, offset = gorder[way][step]
                where = combined.at[c, h, at_z(offset)]
                gring[c, way, step - 2] = send(
                    where, where, beside[way][0], gring_send.at[c, way, step - 2], gring_recv.at[c, way, step - 2]
                )
        if pace == 1:
            for h in range(2):
                gpairs[c, h].wait_recv()
            shift_row(c, 0)

    def gather_end(c):
        for step in (inner, inner + 1):
            for way in range(2):
                landed(c, way, step)

    def masked(c, r):
        if r == ROWS:
            return next_row[c].reshape(plane, n4) * mask23[...]
        return combined[c, r % 2, :, :, r // 2].reshape(plane, n4) * mask23[...]

    def restore(c, r, flat):
        hi, lo = split(flat)
        flat = dot(hi, back4[...]) + dot(lo, back4[...])
        hi, lo = split(flat)
        flat = (dot(back23[c], hi) + dot(back23[c], lo)).reshape(half, n3, n4)
        if c == 0:
            restored[r] = flat
        else:
            out[0, r, :half] = restored[r] + flat
            out[0, r, half:] = restored[r] - flat

    def restore_unit(c):
        restore(c, 0, masked(c, 0))
        for copy in shifted[c].values():
            copy.wait_recv()
        evolved[4] = masked(c, 4).reshape(half, n3, n4)
        evolved[2] = (kept_row[2] * masked(c, 2) + 0.5 * (masked(c, 0) + evolved_row(4))).reshape(half, n3, n4)
        restore(c, 2, evolved_row(2))
        restore(c, 1, kept_row[1] * masked(c, 1) + 0.5 * (masked(c, 0) + evolved_row(2)))
        restore(c, 3, kept_row[3] * masked(c, 3) + 0.5 * (evolved_row(2) + evolved_row(4)))

    evolve_start(0)
    for d in range(DEGREE):
        evolve_step(0, d)
        if d == 2:
            send_own(1)
    evolve_end(0)
    scatter_round(0, 0)
    evolve_start(1)
    for d in range(DEGREE):
        evolve_step(1, d)
        if d == 2:
            scatter_round(0, 1)
        if d == 4:
            scatter_round(0, 2)
    evolve_end(1)
    scatter_round(1, 0)
    scatter_round(0, 3)
    scatter_round(1, 1)
    gather_round(0, 0)
    scatter_round(1, 2)
    gather_round(0, 1)
    scatter_round(1, 3)
    gather_round(0, 2)
    gather_round(1, 0)
    gather_round(0, 3)
    gather_round(1, 1)
    gather_end(0)
    restore_unit(0)
    gather_round(1, 2)
    gather_round(1, 3)
    gather_end(1)
    restore_unit(1)

    started = (high, low, ring, ends, pairs, first, gpairs, gring, *shifted)
    for copy in (copy for group in started for copy in group.values()):
        copy.wait_send()


def shards(fields, cutoffs, weights, diffusion, courant):
    n2, n3, n4 = fields.shape[2:]
    half = n2 // 2
    plane = half * n3
    row = (half, n3, n4)
    tile = (2, n3 // 2, n4)
    dma = pltpu.SemaphoreType.DMA
    return pl.pallas_call(
        functools.partial(kernel, (n2, n3, n4)),
        out_shape=jax.ShapeDtypeStruct(fields.shape, F32),
        in_specs=[pl.BlockSpec(memory_space=pltpu.SMEM)] * 4 + [pl.BlockSpec(memory_space=pl.ANY)],
        out_specs=pl.BlockSpec(memory_space=pltpu.VMEM),
        scratch_shapes=[
            pltpu.VMEM((ROWS, n2, n3, n4), F32),
            pltpu.VMEM((2, WINDOW, *row), F32),
            pltpu.VMEM((ROWS + 1, half + 2, n3, n4), F32),
            pltpu.VMEM((ROWS + 1, half + 2, n3, n4), F32),
            pltpu.VMEM((plane, n4), F32),
            pltpu.VMEM((ROWS + 1, *row), F32),
            pltpu.VMEM((2, 2, half, 2, *tile), F32),
            pltpu.VMEM((2, 2, 5, 2, *tile), F32),
            pltpu.VMEM((2, 2, 2, 2, *tile), F32),
            pltpu.VMEM((2, 2, *tile), F32),
            pltpu.VMEM((2, 2, half, 2, *tile), F32),
            pltpu.VMEM((2, half, *tile), F32),
            pltpu.VMEM((ROWS, *row), F32),
            pltpu.VMEM((n4, n4), BF16),
            pltpu.VMEM((n4, n4), BF16),
            pltpu.VMEM((n4, n4), BF16),
            pltpu.VMEM((2, plane, plane), BF16),
            pltpu.VMEM((n4, n4), BF16),
            pltpu.VMEM((2, plane, plane), BF16),
            pltpu.VMEM((plane, n4), F32),
            dma, dma((2, LOW)), dma((2, LOW)), dma((2, HIGH)), dma((2, HIGH)),
            dma((2, 2, 5)), dma((2, 2, 5)), dma((2, 2, 2, 2)), dma((2, 2, 2, 2)), dma((2, 2)), dma((2, 2)),
            dma((2, 2, 2, 2)), dma((2, 2, 2, 2)), dma((2, 2)), dma((2, 2)), dma((2, 2, 5)), dma((2, 2, 5)),
            dma((2, 8)), dma((2, 8)),
        ],
        compiler_params=pltpu.CompilerParams(
            collective_id=0, has_side_effects=True, vmem_limit_bytes=52 * 1024 * 1024
        ),
        name="advect_combine",
    )(cutoffs, weights, diffusion, courant, fields)


def solution(mesh):
    in_specs = (P("grid", "dom", None, None, None), P("grid", None), P("grid"), P(), P())
    out_specs = P("grid", "dom", None, None, None)
    return jax.shard_map(shards, mesh=mesh, in_specs=in_specs, out_specs=out_specs, check_vma=False)
```

time: 67.2 us -> 69.8 us (1.039); the launches traced: 66.2 us -> 69.7 us
  Pallas kernels: 64.5 us -> 68 us
    pallas_call x1, Pallas kernels: 64.5 us -> 68 us  [shards(): pl.pallas_call(functools.partial(kernel, (n2, n3, n4)), out_shape=jax.Sha...]
where the time goes in v3:
time: 69.8 us; the launch traced here: 69.7 us
  Pallas kernels  68 us (97%)
  local copies, waits for them, and re-layouts  0.98 us (1%)
  between operations  0.73 us (1%)
    pallas_call x1, Pallas kernels, shards(): pl.pallas_call(functools.partial(kernel, (n2, n3, n4)), out_shape=jax.Sha...  68 us

profile of v3, /device:TPU:1, one launch (start us, length us, event | category | flops | bytes accessed | tf_op | source)
XLA Modules:
  0.0 69.7 jit_solution(17340716567945836529)
XLA Ops:
  0.0 0.0 copy-start.2
  0.0 0.0 copy-start.1
  0.0 0.0 copy-start
  0.7 0.0 copy-done.2
  0.7 0.0 copy-done.1
  0.7 0.0 copy-done
  0.7 68.0 %advect_combine.1 = f32[1,4,16,16,256]{4,3,2,1,0:T(8,128)S(1)} custom-call(s32[1,4]{1,0:T(1,128)S(1)} %copy-done, s32[1]{0:T(128)S(6)} %copy.7.weights, f32[4]{0:T(128)S(1)} %copy-done.1, f32[4]{0:T(128)S(1)} %copy-done.2, f32[1,4,16,16,256]{4,3,2,1,0:T(8,128)} %fields.1), custom_call_target="tpu_custom_call" | custom-call | tf_op jit(solution)/shard_map/advect_combine/pallas_call | solution.py:407
  68.7 1.0 %copy.8 = f32[1,4,16,16,256]{4,3,2,1,0:T(8,128)} copy(f32[1,4,16,16,256]{4,3,2,1,0:T(8,128)S(1)} %advect_combine.1) | data formatting | bytes 2097152
Async XLA Ops:
  0.0 0.7 %copy-start.2 = (f32[4]{0:T(128)S(1)}, f32[4]{0:T(128)}, u32[]{:S(2)}) copy-start(f32[4]{0:T(128)} %courant.1) | copy-start | bytes 52
  0.0 0.7 %copy-start.1 = (f32[4]{0:T(128)S(1)}, f32[4]{0:T(128)}, u32[]{:S(2)}) copy-start(f32[4]{0:T(128)} %diffusion.1) | copy-start | bytes 52
  0.0 0.7 %copy-start = (s32[1,4]{1,0:T(1,128)S(1)}, s32[1,4]{1,0:T(1,128)}, u32[]{:S(2)}) copy-start(s32[1,4]{1,0:T(1,128)} %cutoffs.1) | copy-start | bytes 52

commit v4 on v2

--- a/solution.py
+++ b/solution.py
@@ -161,7 +161,7 @@
                 low_send.at[ROWS + d], low_recv.at[ROWS + d],
             )
 
-    def level(d, first, stride, count):
+    def level(d, first, stride, count, missing=None):
         m = DEGREE - d
         now, then = (held_a, held_b) if d % 2 == 0 else (held_b, held_a)
 
@@ -173,6 +173,8 @@
             for i in range(0, n2, block):
                 total = None
                 for j in range(-d, d + 1):
+                    if j == missing:
+                        continue
                     term = q[m, j] * window[LOW + r + j, i : i + block]
                     total = term if total is None else total + term
                 if d > 0:
@@ -195,14 +197,22 @@
             lax.fori_loop(0, count, row, 0)
 
     level(0, 1, 1, 2)
-    for d in range(DEGREE):
+    for d in range(DEGREE - 1):
         level(d, 0, 3, 2)
         level(d + 1, 1, 1, 2)
         if d > 0:
             level(d - 1, 4, 1, 1)
         wait_high(d)
         wait_low(d)
-    level(DEGREE, 0, 3, 2)
+    level(DEGREE - 1, 0, 3, 2)
+    level(DEGREE, 1, 1, 2)
+    level(DEGREE - 2, 4, 1, 1)
+
+    level(DEGREE, 0, 1, 1, -DEGREE)
+    level(DEGREE, 3, 1, 1, DEGREE)
+
+    def farthest(r, j):
+        evolved[r] = evolved[r] + q[0, j] * window[LOW + r + j]
 
     def surplus_of(r, flat):
         hi, lo = split(flat)
@@ -313,12 +323,17 @@
             for way in range(2):
                 landed(c, way, step)
 
+    wait_low(DEGREE - 1)
+    farthest(0, -DEGREE)
     surplus_of(0, evolved_row(0))
     surplus_of(1, evolved_row(1) - 0.5 * (evolved_row(0) + evolved_row(2)))
     scatter_round(0, 0)
+    wait_high(DEGREE - 1)
+    farthest(3, DEGREE)
     level(DEGREE - 1, 4, 1, 1)
+    level(DEGREE, 4, 1, 1, DEGREE)
     wait_high(DEGREE)
-    level(DEGREE, 4, 1, 1)
+    farthest(4, DEGREE)
     surplus_of(2, evolved_row(2) - 0.5 * (evolved_row(0) + evolved_row(4)))
     surplus_of(3, evolved_row(3) - 0.5 * (evolved_row(2) + evolved_row(4)))
     scatter_round(1, 0)

time: 67.2 us -> 66.2 us (0.985); the launches traced: 66.2 us -> 66 us
  no operation moved by 1% of the time
where the time goes in v4:
time: 66.2 us; the launch traced here: 66 us
  Pallas kernels  64.3 us (97%)
  local copies, waits for them, and re-layouts  0.98 us (1%)
  between operations  0.73 us (1%)
    pallas_call x1, Pallas kernels, shards(): pl.pallas_call(functools.partial(kernel, row), out_shape=jax.ShapeDtypeSt...  64.3 us

profile of v4, /device:TPU:1, one launch (start us, length us, event | category | flops | bytes accessed | tf_op | source)
XLA Modules:
  0.0 66.0 jit_solution(3575974048471756958)
XLA Ops:
  0.0 0.0 copy-start.2
  0.0 0.0 copy-start.1
  0.0 0.0 copy-start
  0.7 0.0 copy-done.2
  0.7 0.0 copy-done.1
  0.7 0.0 copy-done
  0.7 64.3 %advect_combine.1 = f32[1,4,16,16,256]{4,3,2,1,0:T(8,128)S(1)} custom-call(s32[1,4]{1,0:T(1,128)S(1)} %copy-done, s32[1]{0:T(128)S(6)} %copy.7.weights, f32[4]{0:T(128)S(1)} %copy-done.1, f32[4]{0:T(128)S(1)} %copy-done.2, f32[1,4,16,16,256]{4,3,2,1,0:T(8,128)} %fields.1), custom_call_target="tpu_custom_call" | custom-call | tf_op jit(solution)/shard_map/advect_combine/pallas_call | solution.py:379
  65.0 1.0 %copy.8 = f32[1,4,16,16,256]{4,3,2,1,0:T(8,128)} copy(f32[1,4,16,16,256]{4,3,2,1,0:T(8,128)S(1)} %advect_combine.1) | data formatting | bytes 2097152
Async XLA Ops:
  0.0 0.7 %copy-start.2 = (f32[4]{0:T(128)S(1)}, f32[4]{0:T(128)}, u32[]{:S(2)}) copy-start(f32[4]{0:T(128)} %courant.1) | copy-start | bytes 52
  0.0 0.7 %copy-start.1 = (f32[4]{0:T(128)S(1)}, f32[4]{0:T(128)}, u32[]{:S(2)}) copy-start(f32[4]{0:T(128)} %diffusion.1) | copy-start | bytes 52
  0.0 0.7 %copy-start = (s32[1,4]{1,0:T(1,128)S(1)}, s32[1,4]{1,0:T(1,128)}, u32[]{:S(2)}) copy-start(s32[1,4]{1,0:T(1,128)} %cutoffs.1) | copy-start | bytes 52

commit v5 on v4

--- a/solution.py
+++ b/solution.py
@@ -85,16 +85,17 @@
     other = lax.rem(base + RING, 2 * RING)
     z_next = (lax.rem(z + 1, RING), lax.rem(z + RING - 1, RING))
     beside = [((base + at, dom_at), (other + at, dom_at)) for at in z_next]
+    two_on = [(base + lax.rem(z + hops, RING), dom_at) for hops in (2, RING - 2)]
     partner = (other + z, dom_at)
     y = base // RING
     y_other = 1 - y
 
     barrier = pltpu.get_barrier_semaphore()
-    for device in ((grid_at, above), (grid_at, below), *beside[0], *beside[1], partner):
+    for device in ((grid_at, above), (grid_at, below), *beside[0], *beside[1], *two_on, partner):
         pl.semaphore_signal(barrier, inc=1, device_id=device, device_id_type=MESH)
     own = pltpu.make_async_copy(fields.at[0], window.at[LOW : LOW + ROWS], own_sem)
     own.start()
-    pl.semaphore_wait(barrier, 7)
+    pl.semaphore_wait(barrier, 9)
 
     def send(source, target, device, send_sem, recv_sem):
         copy = pltpu.make_async_remote_copy(
@@ -233,22 +234,25 @@
 
     order = [[(0, 4), (1, 3), (0, 3), (1, 2), (0, 2), (1, 1), (0, 1)]]
     order.append([(1 - h, -o) for h, o in order[0]])
-    gorder = [[(0, 0), (1, 0), (0, -1), (1, -1), (0, -2), (1, -2), (0, -3)]]
+    rounds = ((0, 2, 1), (4, 3), (6, 5))
+    feeds = {3: (1,), 4: (0, 2), 5: (3,), 6: (4,)}
+    gorder = [[(0, 0), (1, 0), (0, -1), (1, -1), (0, -2), (1, -2), (0, -2)]]
     gorder.append([(1 - h, -o) for h, o in gorder[0]])
-    steps, inner = len(order[0]), len(order[0]) - 2
+    grounds = ((0, 1), (2, 3), (6, 4, 5))
+    inner, skip = 5, 6
     ring, ends, pairs, first, gpairs, gring, shifted = {}, {}, {}, {}, {}, {}, []
 
     def scatter_round(c, pace):
-        for step in range(2 * pace, min(2 * pace + 2, steps)):
+        for step in rounds[pace]:
             for way in range(2):
                 h, offset = order[way][step]
                 where = piece(c, h, offset)
-                if step >= 2:
-                    ring[c, way, step - 2].wait_recv()
-                    surplus[where] = surplus[where] + arrived[c, way, step - 2]
+                for feed in feeds.get(step, ()):
+                    ring[c, way, feed].wait_recv()
+                    surplus[where] = surplus[where] + arrived[c, way, feed]
                 if step < inner:
                     ring[c, way, step] = send(
-                        surplus.at[where], arrived.at[c, way, step], beside[way][0],
+                        surplus.at[where], arrived.at[c, way, step], two_on[way] if step == 0 else beside[way][0],
                         ring_send.at[c, way, step], ring_recv.at[c, way, step],
                     )
                     continue
@@ -290,7 +294,7 @@
         else:
             gring[c, way, step - 2].wait_recv()
         if c == 0 and h == 0:
-            shift_row(offset - (1 - 2 * way))
+            shift_row(offset - (1 - 2 * way) * (2 if step == skip else 1))
 
     def gather_round(c, pace):
         if pace == 0:
@@ -305,12 +309,14 @@
                         )
                 gpairs[c, h] = send(mine, mine, partner, gpair_send.at[c, h], gpair_recv.at[c, h])
             return
-        for step in range(2 * pace, min(2 * pace + 2, steps)):
+        for step in grounds[pace]:
             for way in range(2):
-                landed(c, way, step - 2)
+                if step != 4:
+                    landed(c, way, step - 2 if step < skip else 2)
                 where = combined.at[piece(c, *gorder[way][step])]
                 gring[c, way, step - 2] = send(
-                    where, where, beside[way][0], gring_send.at[c, way, step - 2], gring_recv.at[c, way, step - 2]
+                    where, where, two_on[way] if step == skip else beside[way][0],
+                    gring_send.at[c, way, step - 2], gring_recv.at[c, way, step - 2],
                 )
         if pace == 1:
             for h in range(2):
@@ -319,7 +325,7 @@
                 shift_row(0)
 
     def gather_end(c):
-        for step in (inner, inner + 1):
+        for step in (4, 5, 6):
             for way in range(2):
                 landed(c, way, step)
 
@@ -337,10 +343,10 @@
     surplus_of(2, evolved_row(2) - 0.5 * (evolved_row(0) + evolved_row(4)))
     surplus_of(3, evolved_row(3) - 0.5 * (evolved_row(2) + evolved_row(4)))
     scatter_round(1, 0)
-    for pace in range(1, 4):
+    for pace in range(1, 3):
         for c in range(2):
             scatter_round(c, pace)
-    for pace in range(4):
+    for pace in range(3):
         for c in range(2):
             gather_round(c, pace)
     gather_end(0)

time: 66.2 us -> 64.7 us (0.977)
  Pallas kernels: 64.3 us -> 62.8 us
    pallas_call x1, Pallas kernels: 64.3 us -> 62.8 us  [shards(): pl.pallas_call(functools.partial(kernel, row), out_shape=jax.ShapeDtypeSt...]
where the time goes in v5:
time: 64.7 us; the launch traced here: 64.5 us
  Pallas kernels  62.8 us (97%)
  local copies, waits for them, and re-layouts  0.98 us (2%)
  between operations  0.73 us (1%)
    pallas_call x1, Pallas kernels, shards(): pl.pallas_call(functools.partial(kernel, row), out_shape=jax.ShapeDtypeSt...  62.8 us

profile of v5, /device:TPU:1, one launch (start us, length us, event | category | flops | bytes accessed | tf_op | source)
XLA Modules:
  0.0 64.5 jit_solution(6724878516448751412)
XLA Ops:
  0.0 0.0 copy-start.2
  0.0 0.0 copy-start.1
  0.0 0.0 copy-start
  0.7 0.0 copy-done.2
  0.7 0.0 copy-done.1
  0.7 0.0 copy-done
  0.7 62.8 %advect_combine.1 = f32[1,4,16,16,256]{4,3,2,1,0:T(8,128)S(1)} custom-call(s32[1,4]{1,0:T(1,128)S(1)} %copy-done, s32[1]{0:T(128)S(6)} %copy.7.weights, f32[4]{0:T(128)S(1)} %copy-done.1, f32[4]{0:T(128)S(1)} %copy-done.2, f32[1,4,16,16,256]{4,3,2,1,0:T(8,128)} %fields.1), custom_call_target="tpu_custom_call" | custom-call | tf_op jit(solution)/shard_map/advect_combine/pallas_call | solution.py:385
  63.5 1.0 %copy.8 = f32[1,4,16,16,256]{4,3,2,1,0:T(8,128)} copy(f32[1,4,16,16,256]{4,3,2,1,0:T(8,128)S(1)} %advect_combine.1) | data formatting | bytes 2097152
Async XLA Ops:
  0.0 0.7 %copy-start.2 = (f32[4]{0:T(128)S(1)}, f32[4]{0:T(128)}, u32[]{:S(2)}) copy-start(f32[4]{0:T(128)} %courant.1) | copy-start | bytes 52
  0.0 0.7 %copy-start.1 = (f32[4]{0:T(128)S(1)}, f32[4]{0:T(128)}, u32[]{:S(2)}) copy-start(f32[4]{0:T(128)} %diffusion.1) | copy-start | bytes 52
  0.0 0.7 %copy-start = (s32[1,4]{1,0:T(1,128)S(1)}, s32[1,4]{1,0:T(1,128)}, u32[]{:S(2)}) copy-start(s32[1,4]{1,0:T(1,128)} %cutoffs.1) | copy-start | bytes 52

commit v6 on v5

--- a/solution.py
+++ b/solution.py
@@ -205,12 +205,10 @@
             level(d - 1, 4, 1, 1)
         wait_high(d)
         wait_low(d)
-    level(DEGREE - 1, 0, 3, 2)
+    level(DEGREE - 1, 0, 1, 1)
     level(DEGREE, 1, 1, 2)
-    level(DEGREE - 2, 4, 1, 1)
 
     level(DEGREE, 0, 1, 1, -DEGREE)
-    level(DEGREE, 3, 1, 1, DEGREE)
 
     def farthest(r, j):
         evolved[r] = evolved[r] + q[0, j] * window[LOW + r + j]
@@ -334,6 +332,9 @@
     surplus_of(0, evolved_row(0))
     surplus_of(1, evolved_row(1) - 0.5 * (evolved_row(0) + evolved_row(2)))
     scatter_round(0, 0)
+    level(DEGREE - 1, 3, 1, 1)
+    level(DEGREE, 3, 1, 1, DEGREE)
+    level(DEGREE - 2, 4, 1, 1)
     wait_high(DEGREE - 1)
     farthest(3, DEGREE)
     level(DEGREE - 1, 4, 1, 1)

time: 64.7 us -> 64.7 us (level)
  no operation moved by 1% of the time
where the time goes in v6:
time: 64.7 us; the launch traced here: 64.6 us
  Pallas kernels  62.9 us (97%)
  local copies, waits for them, and re-layouts  0.98 us (2%)
  between operations  0.73 us (1%)
    pallas_call x1, Pallas kernels, shards(): pl.pallas_call(functools.partial(kernel, row), out_shape=jax.ShapeDtypeSt...  62.9 us

profile of v6, /device:TPU:1, one launch (start us, length us, event | category | flops | bytes accessed | tf_op | source)
XLA Modules:
  0.0 64.6 jit_solution(12156635026883791903)
XLA Ops:
  0.0 0.0 copy-start.2
  0.0 0.0 copy-start.1
  0.0 0.0 copy-start
  0.7 0.0 copy-done.2
  0.7 0.0 copy-done.1
  0.7 0.0 copy-done
  0.7 62.9 %advect_combine.1 = f32[1,4,16,16,256]{4,3,2,1,0:T(8,128)S(1)} custom-call(s32[1,4]{1,0:T(1,128)S(1)} %copy-done, s32[1]{0:T(128)S(6)} %copy.7.weights, f32[4]{0:T(128)S(1)} %copy-done.1, f32[4]{0:T(128)S(1)} %copy-done.2, f32[1,4,16,16,256]{4,3,2,1,0:T(8,128)} %fields.1), custom_call_target="tpu_custom_call" | custom-call | tf_op jit(solution)/shard_map/advect_combine/pallas_call | solution.py:386
  63.6 1.0 %copy.8 = f32[1,4,16,16,256]{4,3,2,1,0:T(8,128)} copy(f32[1,4,16,16,256]{4,3,2,1,0:T(8,128)S(1)} %advect_combine.1) | data formatting | bytes 2097152
Async XLA Ops:
  0.0 0.7 %copy-start.2 = (f32[4]{0:T(128)S(1)}, f32[4]{0:T(128)}, u32[]{:S(2)}) copy-start(f32[4]{0:T(128)} %courant.1) | copy-start | bytes 52
  0.0 0.7 %copy-start.1 = (f32[4]{0:T(128)S(1)}, f32[4]{0:T(128)}, u32[]{:S(2)}) copy-start(f32[4]{0:T(128)} %diffusion.1) | copy-start | bytes 52
  0.0 0.7 %copy-start = (s32[1,4]{1,0:T(1,128)S(1)}, s32[1,4]{1,0:T(1,128)}, u32[]{:S(2)}) copy-start(s32[1,4]{1,0:T(1,128)} %cutoffs.1) | copy-start | bytes 52
